TPU v7x, 32 devices: a whole 2x2x4 slice. The times are simulated.
32 devices in a mesh: wide: 8 (over z, y), lev: 4 (over x, core).
Axes of the slice: x: 2, y: 2, z: 4, core: 2. Of those that a mesh axis runs over, the one named last changes fastest.
Arguments:
- nonlinear: bfloat16 [3, 2, 256, 8, 4096], P(None, None, 'lev', None, 'wide'), may hold values from -20 to 20
Outputs:
- pressure: float32 [2, 256, 8, 1536], P(None, 'lev', 'wide')
All inputs are finite; a program needn't handle non-finite values.
Results may differ from a plain program's by a relative error of at most 0.0034.
Values may be sent and summed in bfloat16 or wider, within the bound.
A program may use at most 64 MiB of HBM per device.

v0:
```python
import math

import jax
import jax.numpy as jnp
from jax import lax
from jax.sharding import PartitionSpec as P

NXG = 4096
KXM = 1536
KY_DEV = 1


def padded_2(cells, sides, width):
    for axis, dim in sides:
        count = lax.axis_size(axis)
        ends = count - 1
        head = lax.slice_in_dim(cells, 0, width, axis=dim)
        tail = lax.slice_in_dim(cells, cells.shape[dim] - width, cells.shape[dim], axis=dim)
        cells = jnp.concatenate(
            [
                lax.ppermute(tail, axis, [(i, (i + 1) % count) for i in range(ends)]),
                cells,
                lax.ppermute(head, axis, [((i + 1) % count, i) for i in range(ends)]),
            ],
            axis=dim,
        )
    return cells


def from_behind(block, axis, distance):
    devices = range(lax.axis_size(axis))
    route = [(i - distance, i) for i in devices if i - distance in devices]
    return lax.ppermute(block, axis, route)


def make_tables():
    places = jnp.arange(NXG, dtype=jnp.int32)
    waves = jnp.arange(KXM, dtype=jnp.int32) - KXM // 2
    phases = jnp.mod(places[:, None] * waves[None, :], NXG)
    angles = phases.astype(jnp.float32) * (2.0 * math.pi / NXG)
    return (jnp.cos(angles).astype(jnp.bfloat16), jnp.sin(angles).astype(jnp.bfloat16))


def wave_scales(first_row, row_count):
    spacing = 2.0 * math.pi / NXG
    ky_scaled = (first_row + jnp.arange(row_count, dtype=jnp.int32)).astype(jnp.float32) * spacing
    kx_scaled = (jnp.arange(KXM, dtype=jnp.int32) - KXM // 2).astype(jnp.float32) * spacing
    return (ky_scaled[:, None], kx_scaled[None, :])


def vertical_mix(y_term, z_padded, ky_scaled):
    upper = z_padded[:, 2:].astype(jnp.float32)
    lower = z_padded[:, :-2].astype(jnp.float32)
    half_diff = (upper - lower) * 0.5
    y_wide = y_term.astype(jnp.float32)
    real_part = half_diff[0] - ky_scaled * y_wide[1]
    imag_part = half_diff[1] + ky_scaled * y_wide[0]
    return jnp.stack([real_part, imag_part]).astype(jnp.bfloat16)


def spectral_source(x_term, g_term, cosine, sine, kx_scaled):
    stacked = jnp.concatenate([x_term, g_term], axis=0)
    lead_shape = stacked.shape[:3]
    flat_rows = stacked.reshape(-1, stacked.shape[3])
    with_cos = jnp.dot(flat_rows, cosine, preferred_element_type=jnp.float32).reshape(
        lead_shape + (cosine.shape[1],)
    )
    with_sin = jnp.dot(flat_rows, sine, preferred_element_type=jnp.float32).reshape(
        lead_shape + (sine.shape[1],)
    )
    norm_scale = 1.0 / math.sqrt(cosine.shape[0])
    fx_real = (with_cos[0] + with_sin[1]) * norm_scale
    fx_imag = (with_cos[1] - with_sin[0]) * norm_scale
    fg_real = (with_cos[2] + with_sin[3]) * norm_scale
    fg_imag = (with_cos[3] - with_sin[2]) * norm_scale
    return jnp.stack([kx_scaled * fx_imag - fg_real, -kx_scaled * fx_real - fg_imag])


def tridiag_sweep(diagonal, source):

    def tridiag_forward_step(previous, row_data):
        shift_coef, prior_value = previous
        inverse = 1.0 / (diagonal + shift_coef)
        reduced_value = (row_data + prior_value) * inverse
        return ((-inverse, reduced_value), (inverse, reduced_value))

    initial = (jnp.zeros_like(diagonal), jnp.zeros_like(source[0]))
    _, (inverses, reduced) = lax.scan(tridiag_forward_step, initial, source)

    def tridiag_backward_step(following, row_pair):
        inverse, reduced_value = row_pair
        result = reduced_value + inverse * following
        return (result, result)

    _, solved = lax.scan(
        tridiag_backward_step, jnp.zeros_like(source[0]), (inverses, reduced), reverse=True
    )
    return solved


def solve_rows(lower_coef, centre_coef, upper_coef, targets):

    def solve_forward_step(previous, row_data):
        ratio_prev, prior_value = previous
        lower_now, centre_now, upper_now, target_now = row_data
        inverse = 1.0 / (centre_now - lower_now * ratio_prev)
        ratio_now = upper_now * inverse
        reduced_value = (target_now - lower_now * prior_value) * inverse
        return ((ratio_now, reduced_value), (ratio_now, reduced_value))

    initial = (jnp.zeros_like(centre_coef[0]), jnp.zeros_like(targets[0]))
    _, (ratios, reduced) = lax.scan(
        solve_forward_step, initial, (lower_coef, centre_coef, upper_coef, targets)
    )

    def solve_backward_step(following, row_pair):
        ratio_now, reduced_value = row_pair
        result = reduced_value - ratio_now * following
        return (result, result)

    _, solved = lax.scan(
        solve_backward_step, jnp.zeros_like(targets[0]), (ratios, reduced), reverse=True
    )
    return solved


def local(nonlinear):
    cosine, sine = make_tables()
    first_row = lax.axis_index("wide") * KY_DEV
    ky_here, kx_scaled = wave_scales(first_row, KY_DEV)
    x_lines = lax.all_to_all(nonlinear, "wide", split_axis=3, concat_axis=4, tiled=True)
    padded = padded_2(x_lines[2], (("lev", 1),), 1)
    combined = vertical_mix(x_lines[1], padded, ky_here)
    source = spectral_source(x_lines[0], combined, cosine, sine, kx_scaled)
    diagonal = 2.0 + (ky_here * ky_here + kx_scaled * kx_scaled)
    levels = jnp.moveaxis(source, 1, 0)
    inner = levels.shape[0] - 1
    level_marks = jnp.arange(inner, dtype=jnp.int32)[:, None, None, None]
    unit_shape = (inner, 1) + diagonal.shape
    first_unit = jnp.broadcast_to((level_marks == 0).astype(jnp.float32), unit_shape)
    last_unit = jnp.broadcast_to((level_marks == inner - 1).astype(jnp.float32), unit_shape)
    local_part = tridiag_sweep(
        diagonal, jnp.concatenate([levels[:inner], first_unit, last_unit], axis=1)
    )
    particular = local_part[:, :2]
    from_above = local_part[:, 2]
    from_below = local_part[:, 3]
    next_particular, next_above, next_below = from_behind(
        (particular[0], from_above[0], from_below[0]), "lev", -1
    )
    lower_coef = -from_above[inner - 1]
    centre_coef = diagonal - from_below[inner - 1] - next_above
    upper_coef = -next_below
    target = levels[inner] + particular[inner - 1] + next_particular
    all_lower, all_centre, all_upper, all_target = (
        lax.all_gather(lower_coef[None], "lev", axis=0, tiled=True),
        lax.all_gather(centre_coef[None], "lev", axis=0, tiled=True),
        lax.all_gather(upper_coef[None], "lev", axis=0, tiled=True),
        lax.all_gather(target[None], "lev", axis=0, tiled=True),
    )
    separators = solve_rows(all_lower, all_centre, all_upper, all_target)
    level_at = lax.axis_index("lev")
    this_sep = lax.dynamic_index_in_dim(separators, level_at, 0, keepdims=False)
    above_raw = lax.dynamic_index_in_dim(
        separators, jnp.maximum(level_at - 1, 0), 0, keepdims=False
    )
    above_sep = jnp.where(level_at > 0, above_raw, 0.0)
    interior = particular + from_above[:, None] * above_sep + from_below[:, None] * this_sep
    pressure = jnp.concatenate([interior, this_sep[None]], axis=0)
    return jnp.moveaxis(pressure, 0, 1)


def solution(mesh):
    placed = (P(None, None, "lev", None, "wide"),)
    return jax.shard_map(
        local, mesh=mesh, in_specs=placed, out_specs=P(None, "lev", "wide", None), check_vma=False
    )
```

profile of v0, /device:TPU:0, one launch (start us, length us, event | category | flops | bytes accessed | tf_op | source)
XLA Modules:
  0.0 541.5 jit_solution(10438381052601873992)
XLA Ops:
  0.0 4.6 copy.18
  4.6 7.3 %all-to-all-start = ((bf16[3,2,64,8,512]{4,2,1,0,3:T(8,128)(2,1)}), bf16[3,2,64,8,512]{4,2,1,0,3:T(8,128)(2,1)S(1)}, u32[]{:S(2)}, u32[]{:S(2)}) async-start(bf16[3,2,64,8,512]{4,2,1,0,3:T(8,128)(2,1)} %copy.18), calls=%async_computation | async-start | bytes 6291456 | tf_op jit(solution)/shard_map/all_to_all | solution.py:131
  12.0 70.6 %all-to-all-done = bf16[3,2,64,8,512]{4,2,1,0,3:T(8,128)(2,1)S(1)} async-done(((bf16[3,2,64,8,512]{4,2,1,0,3:T(8,128)(2,1)}), bf16[3,2,64,8,512]{4,2,1,0,3:T(8,128)(2,1)S(1)}, u32[]{:S(2)}, u32[]{:S(2)}) %all-to-all-start) | async-done | bytes 3145760 | tf_op jit(solution)/shard_map/all_to_all | solution.py:131
  82.6 2.1 fusion.56
  84.7 1.6 copy.20
  86.2 1.6 squeeze.79
  87.9 1.3 collective-permute-start
  89.2 3.0 collective-permute-start.1
  92.2 1.3 slice_multiply_fusion.1
  94.3 2.9 copy.23
  97.2 2.4 mul.292
  99.6 1.6 copy.19
  101.2 1.6 squeeze.78
  104.5 93.1 %fusion.22 = f32[256,1536]{1,0:T(8,128)S(1)} fusion(bf16[256,4096]{1,0:T(8,128)(2,1)S(1)} %bitcast.114, s32[1536]{0:T(1024)S(1)} %iota_add_fusion), kind=kOutput, calls=%fused_computation.42 | convolution fusion | flops 3315597312 | bytes 3676160 | tf_op jit(solution)/shard_map/dot_general | solution.py:65
  197.6 105.1 %fusion.23 = f32[256,1536]{1,0:T(8,128)S(1)} fusion(bf16[256,4096]{1,0:T(8,128)(2,1)S(1)} %bitcast.115, s32[1536]{0:T(1024)S(1)} %iota_add_fusion), kind=kOutput, calls=%fused_computation.43 | convolution fusion | flops 3315597312 | bytes 3676160 | tf_op jit(solution)/shard_map/dot_general | solution.py:68
  303.2 1.3 pad_maximum_fusion.1
  305.3 104.9 %while.68 = (s32[]{:T(128)}, f32[1,1536]{1,0:T(1,128)S(1)}, f32[4,1,1536]{2,1,0:T(1,128)S(1)}, f32[63,1,1536]{2,1,0:T(1,128)}, f32[63,4,1,1536]{3,2,1,0:T(1,128)...) while((s32[]{:T(128)}, f32[1,1536]{1,0:T(1,128)S(1)}, ...), condition=%wide.region_1.2_spmd.clone, body=%wide.region_0.1_spmd.clone.sunk | while | flops 33795 | bytes 144492 | solution.py:88
  307.6 1.0 bitcast_dynamic-update-slice_fusion.13
  310.9 1.0 bitcast_dynamic-update-slice_fusion.13
  314.3 1.0 bitcast_dynamic-update-slice_fusion.13
  315.9 1.0 bitcast_dynamic-update-slice_fusion.13
  317.6 1.0 bitcast_dynamic-update-slice_fusion.13
  319.3 1.0 bitcast_dynamic-update-slice_fusion.13
  320.9 1.0 bitcast_dynamic-update-slice_fusion.13
  322.6 1.0 bitcast_dynamic-update-slice_fusion.13
  325.9 1.0 bitcast_dynamic-update-slice_fusion.13
  329.3 1.0 bitcast_dynamic-update-slice_fusion.13
  332.6 1.0 bitcast_dynamic-update-slice_fusion.13
  335.9 1.0 bitcast_dynamic-update-slice_fusion.13
  339.3 1.0 bitcast_dynamic-update-slice_fusion.13
  342.6 1.0 bitcast_dynamic-update-slice_fusion.13
  345.9 1.0 bitcast_dynamic-update-slice_fusion.13
  347.6 1.0 bitcast_dynamic-update-slice_fusion.13
  349.2 1.0 bitcast_dynamic-update-slice_fusion.13
  350.9 1.0 bitcast_dynamic-update-slice_fusion.13
  352.6 1.0 bitcast_dynamic-update-slice_fusion.13
  354.2 1.0 bitcast_dynamic-update-slice_fusion.13
  357.6 1.0 bitcast_dynamic-update-slice_fusion.13
  360.9 1.0 bitcast_dynamic-update-slice_fusion.13
  364.2 1.0 bitcast_dynamic-update-slice_fusion.13
  367.6 1.0 bitcast_dynamic-update-slice_fusion.13
  370.9 1.0 bitcast_dynamic-update-slice_fusion.13
  374.2 1.0 bitcast_dynamic-update-slice_fusion.13
  377.6 1.0 bitcast_dynamic-update-slice_fusion.13
  379.2 1.0 bitcast_dynamic-update-slice_fusion.13
  380.9 1.0 bitcast_dynamic-update-slice_fusion.13
  382.6 1.0 bitcast_dynamic-update-slice_fusion.13
  384.2 1.0 bitcast_dynamic-update-slice_fusion.13
  385.9 1.0 bitcast_dynamic-update-slice_fusion.13
  389.2 1.0 bitcast_dynamic-update-slice_fusion.13
  392.6 1.0 bitcast_dynamic-update-slice_fusion.13
  395.9 1.0 bitcast_dynamic-update-slice_fusion.13
  399.2 1.0 bitcast_dynamic-update-slice_fusion.13
  402.6 1.0 bitcast_dynamic-update-slice_fusion.13
  410.2 1.2 copy-done.3
  412.2 97.0 %while.69 = (s32[]{:T(128)}, f32[4,1,1536]{2,1,0:T(1,128)S(1)}, f32[63,4,1,1536]{3,2,1,0:T(1,128)S(1)}, f32[63,4,1,1536]{3,2,1,0:T(1,128)}, f32[63,1,1536]{2,1,0:T(1,128)}, /*index=5*/s32[]{:T(128)}, s32[]{:T(128)}, s32[]{:T(128)}) while((s32[]{:T(128)}, f32[4,1,1536]{2,1,0:T(1,128)S(1)}, f32[63,4,1,1536]{3,2,1,0:T(1,128)S(1)}, ...), condition=%wide.region_3.4_spmd.clone, body=%wide.region_2.3_spmd.clone.sunk | while | flops 18436 | bytes 118899 | solution.py:95
  509.8 1.3 collective-permute-start.4
  511.1 1.3 collective-permute-start.3
  512.4 1.3 collective-permute-start.2
  513.8 8.3 %all-gather.2 = f32[4,1,1,1536]{3,2,1,0:T(1,128)S(1)} all-gather(f32[1,1,1,1536]{3,2,1,0:T(1,128)S(1)} %get-tuple-element.496), channel_id=4, replica_groups=mesh['wide'=8,'lev'=4] {'lev'}, dimensions={0}, use_global_device_ids=true | all-gather | bytes 30720 | tf_op jit(solution)/shard_map/all_gather | solution.py:156
  522.1 5.2 all-gather.5
  527.3 5.2 all-gather.4
  532.5 5.2 all-gather.3
  539.7 1.6 maximum_bitcast_fusion.1
  (352 shorter events, 170.7 us)
Async XLA Ops:
  4.6 78.0 %all-to-all-start = ((bf16[3,2,64,8,512]{4,2,1,0,3:T(8,128)(2,1)}), bf16[3,2,64,8,512]{4,2,1,0,3:T(8,128)(2,1)S(1)}, u32[]{:S(2)}, u32[]{:S(2)}) async-start(bf16[3,2,64,8,512]{4,2,1,0,3:T(8,128)(2,1)} %copy.18), calls=%async_computation | async-start | bytes 6291456 | tf_op jit(solution)/shard_map/all_to_all | solution.py:131
  84.7 7.5 %copy-start = (f32[1,2,64,8,512]{4,2,1,0,3:T(8,128)S(1)}, f32[1,2,64,8,512]{4,2,1,0,3:T(8,128)}, u32[]{:S(2)}) copy-start(f32[1,2,64,8,512]{4,2,1,0,3:T(8,128)} %get-tuple-element.488) | copy-start | bytes 6291460
  87.9 14.9 %collective-permute-start = (bf16[2,1,1,4096]{3,1,0,2:T(2,128)(2,1)S(1)}, bf16[2,1,1,4096]{3,1,0,2:T(2,128)(2,1)S(1)}, u32[]{:S(2)}, u32[]{:S(2)}) collective-permute-start(bf16[2,1,1,4096]{3,1,0,2:T(2,128)(2,1)S(1)} %get-tuple-element.499), channel_id=1, source_target_pairs={{1,0},{2,1},{3,2},{5,4},{6,5},{7,6},{9,8},{10,9},{11,10},{13,12},{... | collective-permute-start | bytes 49160 | tf_op jit(solution)/shard_map/ppermute | solution.py:23
  89.2 13.6 %collective-permute-start.1 = (bf16[2,1,1,4096]{3,1,0,2:T(2,128)(2,1)S(1)}, bf16[2,1,1,4096]{3,1,0,2:T(2,128)(2,1)S(1)}, u32[]{:S(2)}, u32[]{:S(2)}) collective-permute-start(bf16[2,1,1,4096]{3,1,0,2:T(2,128)(2,1)S(1)} %get-tuple-element.500), channel_id=1, source_target_pairs={{0,1},{1,2},{2,3},{4,5},{5,6},{6,7},{8,9},{9,10},{10,11},{12,13},{... | collective-permute-start | bytes 49160 | tf_op jit(solution)/shard_map/ppermute | solution.py:21
  94.3 5.3 copy-start.1
  102.8 1.2 copy-start.2
  410.2 1.2 copy-start.3
  509.8 22.7 %collective-permute-start.4 = (f32[2,1,1536]{2,1,0:T(1,128)S(1)}, f32[2,1,1536]{2,1,0:T(1,128)S(1)}, u32[]{:S(2)}, u32[]{:S(2)}) collective-permute-start(f32[2,1,1536]{2,1,0:T(1,128)S(1)} %slice_bitcast_fusion), channel_id=1, source_target_pairs={{1,0},{2,1},{3,2},{5,4},{6,5},{7,6},{9,8},{10,9},{11,10},{13,12},{... | collective-permute-start | bytes 36872 | tf_op jit(solution)/shard_map/ppermute | solution.py:33
  511.1 10.9 %collective-permute-start.3 = (f32[1,1536]{1,0:T(1,128)S(1)}, f32[1,1536]{1,0:T(1,128)S(1)}, u32[]{:S(2)}, u32[]{:S(2)}) collective-permute-start(f32[1,1536]{1,0:T(1,128)S(1)} %get-tuple-element.497), channel_id=1, source_target_pairs={{1,0},{2,1},{3,2},{5,4},{6,5},{7,6},{9,8},{10,9},{11,10},{13,12},{... | collective-permute-start | bytes 18440 | tf_op jit(solution)/shard_map/ppermute | solution.py:33
  512.4 9.7 %collective-permute-start.2 = (f32[1,1536]{1,0:T(1,128)S(1)}, f32[1,1536]{1,0:T(1,128)S(1)}, u32[]{:S(2)}, u32[]{:S(2)}) collective-permute-start(f32[1,1536]{1,0:T(1,128)S(1)} %get-tuple-element.498), channel_id=1, source_target_pairs={{1,0},{2,1},{3,2},{5,4},{6,5},{7,6},{9,8},{10,9},{11,10},{13,12},{... | collective-permute-start | bytes 18440 | tf_op jit(solution)/shard_map/ppermute | solution.py:33
where the time goes:
time: 549 us; the launch traced here: 542 us
  matrix products  198 us (36%)
  other arithmetic  164 us (30%)
  waiting for transfers between devices  70.6 us (13%)
  local copies, waits for them, and re-layouts  66.6 us (12%)
  blocking collectives  23.9 us (4%)
  starting transfers between devices  15.5 us (3%)
    dynamic_update_slice x189, other arithmetic, tridiag_sweep(): _, (inverses, reduced) = lax.scan(tridiag_forward_step, initial, source)  153 us
    dot_general x1, matrix products, spectral_source(): jnp.dot(flat_rows, sine, preferred_element_type=jnp.float32)  105 us
    dot_general x1, matrix products, spectral_source(): jnp.dot(flat_rows, cosine, preferred_element_type=jnp.float32)  93.1 us
    all_to_all x1, waiting for transfers between devices, local(): lax.all_to_all(nonlinear, 'wide', split_axis=3, concat_axis=4, tiled=True)  70.6 us
    dynamic_slice x63, local copies, waits for them, and re-layouts, tridiag_sweep(): lax.scan(tridiag_backward_step, jnp.zeros_like(source[0]), (inverses, red...  45.1 us
  transfers between devices with their start and end apart: 6, of which 1 were waited for; matrix products, arithmetic and copies ran while one was open for 2% of the time, Pallas kernels for 0%

commit v1 on v0

v1 whole, which is shorter than its diff:
```python
import functools
import math

import jax
import jax.numpy as jnp
import ml_dtypes
import numpy as np
from jax import lax
from jax.experimental import pallas as pl
from jax.experimental.pallas import tpu as pltpu
from jax.sharding import PartitionSpec as P

NXG = 4096
KXM = 1536
MESH = pl.DeviceIdType.MESH
COLS = 512


def make_tables():
    places = np.arange(NXG, dtype=np.int32)
    waves = np.arange(KXM, dtype=np.int32) - KXM // 2
    phases = np.mod(places[:, None] * waves[None, :], NXG)
    turn = np.arange(NXG, dtype=np.float32) * np.float32(2.0 * math.pi / NXG)
    cosine = np.cos(turn).astype(ml_dtypes.bfloat16)[phases]
    sine = np.sin(turn).astype(ml_dtypes.bfloat16)[phases]
    return np.concatenate([cosine, sine], axis=1)


def partner(me, step, count):
    total, unit = 0, 1
    while unit < count:
        total = total + unit * ((me // unit + step // unit) % 2)
        unit *= 2
    return total


def kernel(
    wide, lev, rows_ky, levels,
    x_ref, tab_ref, out_ref,
    tab, send, recv, halo_lo, halo_hi, zpad, acc, coef, from_lo, from_hi, part,
    ends, last_val, first_val,
    tab_sem, halo_send, halo_recv, send_sem, recv_sem, end_send, end_recv,
):
    chunk = x_ref.shape[3]
    line_rows = levels * rows_ky
    half = 2 * levels
    group_levels = max(16, 256 // rows_ky)
    group_rows = group_levels * rows_ky
    groups = levels // group_levels
    halo_rows = halo_lo.shape[1]
    me = lax.axis_index("wide")
    block = lax.axis_index("lev")

    tab_parts = tab_sem.shape[0]
    tab_rows = NXG // tab_parts

    def tab_copy(i):
        rows = pl.ds(i * tab_rows, tab_rows)
        return pltpu.make_async_copy(tab_ref.at[rows], tab.at[rows], tab_sem.at[i])

    barrier = pltpu.get_barrier_semaphore()
    for step in range(1, wide):
        pl.semaphore_signal(
            barrier, inc=1, device_id={"wide": partner(me, step, wide)}, device_id_type=MESH
        )
    for step in range(1, lev):
        pl.semaphore_signal(
            barrier, inc=1, device_id={"lev": (block + step) % lev}, device_id_type=MESH
        )
    pl.semaphore_wait(barrier, wide + lev - 2)

    to_prev = pltpu.make_async_remote_copy(
        src_ref=x_ref.at[2, :, 0:halo_rows],
        dst_ref=halo_hi,
        send_sem=halo_send.at[0],
        recv_sem=halo_recv.at[0],
        device_id={"lev": (block + lev - 1) % lev},
        device_id_type=MESH,
    )
    to_next = pltpu.make_async_remote_copy(
        src_ref=x_ref.at[2, :, line_rows - halo_rows:line_rows],
        dst_ref=halo_lo,
        send_sem=halo_send.at[1],
        recv_sem=halo_recv.at[1],
        device_id={"lev": (block + 1) % lev},
        device_id_type=MESH,
    )
    to_prev.start()
    to_next.start()

    out_row = lax.broadcasted_iota(jnp.int32, (group_rows, group_rows), 0)
    in_row = lax.broadcasted_iota(jnp.int32, (group_rows, group_rows), 1)
    wanted = (out_row % group_levels) * rows_ky + out_row // group_levels
    shuffle = jnp.where(in_row == wanted, 1.0, 0.0).astype(jnp.bfloat16)

    def place(values, first):
        moved = jnp.dot(shuffle, values, preferred_element_type=jnp.float32).astype(jnp.bfloat16)
        for ky in range(rows_ky):
            send[ky, first:first + group_levels, :] = moved[
                ky * group_levels:(ky + 1) * group_levels
            ]

    def line_copy(step, which):
        other = partner(me, step, wide)
        rows = pl.ds(which * half, half)
        return pltpu.make_async_remote_copy(
            src_ref=send.at[other, rows],
            dst_ref=recv.at[me, rows],
            send_sem=send_sem.at[which, step],
            recv_sem=recv_sem.at[which, step],
            device_id={"wide": other},
            device_id_type=MESH,
        )

    def line_arrival(step, which):
        other = partner(me, step, wide)
        rows = pl.ds(which * half, half)
        return pltpu.make_async_remote_copy(
            src_ref=send.at[other, rows],
            dst_ref=recv.at[other, rows],
            send_sem=send_sem.at[which, step],
            recv_sem=recv_sem.at[which, step],
            device_id={"wide": other},
            device_id_type=MESH,
        )

    for c in range(2):
        for g in range(groups):
            place(
                x_ref[0, c, g * group_rows:(g + 1) * group_rows, :],
                c * levels + g * group_levels,
            )
    for step in range(wide - 1, 0, -1):
        line_copy(step, 0).start()

    for i in range(tab_parts):
        tab_copy(i).start()

    for c in range(2):
        zpad[c, rows_ky:rows_ky + line_rows, :] = x_ref[2, c].astype(jnp.float32)
    to_prev.wait_recv()
    to_next.wait_recv()
    for c in range(2):
        low = halo_lo[c].astype(jnp.float32)[halo_rows - rows_ky:]
        high = halo_hi[c].astype(jnp.float32)[:rows_ky]
        zpad[c, 0:rows_ky, :] = jnp.where(block > 0, low, 0.0)
        zpad[c, rows_ky + line_rows:, :] = jnp.where(block < lev - 1, high, 0.0)
    spacing = 2.0 * math.pi / NXG
    ky_row = lax.broadcasted_iota(jnp.int32, (group_rows, chunk), 0) % rows_ky
    ky_scaled = ky_row.astype(jnp.float32) * spacing
    for c in range(2):
        for g in range(groups):
            at = g * group_rows
            upper = zpad[c, at + 2 * rows_ky:at + 2 * rows_ky + group_rows, :]
            lower = zpad[c, at:at + group_rows, :]
            turned = ky_scaled * x_ref[1, 1 - c, at:at + group_rows, :].astype(jnp.float32)
            slope = (upper - lower) * 0.5
            mixed = slope - turned if c == 0 else slope + turned
            place(mixed.astype(jnp.bfloat16), half + c * levels + g * group_levels)
    for step in range(wide - 1, 0, -1):
        line_copy(step, 1).start()

    kx_scaled = (
        lax.broadcasted_iota(jnp.int32, (1, KXM), 1) - KXM // 2
    ).astype(jnp.float32) * spacing
    ky_here = me.astype(jnp.float32) * spacing
    diagonal = 2.0 + (ky_here * ky_here + kx_scaled * kx_scaled)

    def coef_step(i, carry):
        shift, gain = carry
        inverse = 1.0 / (diagonal - shift)
        gain = gain * inverse
        coef[pl.ds(i, 1), :] = inverse
        from_lo[pl.ds(i, 1), :] = gain
        return inverse, gain

    zeros = jnp.zeros((1, KXM), jnp.float32)
    ones = jnp.ones((1, KXM), jnp.float32)
    lax.fori_loop(0, levels, coef_step, (zeros, ones))

    def unit_step(j, carry):
        i = levels - 1 - j
        low, high = carry
        inverse = coef[pl.ds(i, 1), :]
        low = from_lo[pl.ds(i, 1), :] + inverse * low
        high = inverse * high
        from_lo[pl.ds(i, 1), :] = low
        from_hi[pl.ds(i, 1), :] = high
        return low, high

    lax.fori_loop(0, levels, unit_step, (zeros, ones))

    for i in range(tab_parts):
        tab_copy(i).wait()

    own_at = pl.multiple_of(me * chunk, chunk)

    @pl.loop(0, 2 * KXM // COLS)
    def _(t):
        cols = pl.ds(pl.multiple_of(t * COLS, COLS), COLS)
        acc[:, cols] = jnp.dot(
            send[me], tab[pl.ds(own_at, chunk), cols], preferred_element_type=jnp.float32
        )

    def chunk_step(step, carry):
        line_arrival(step, 0).wait_recv()
        line_arrival(step, 1).wait_recv()
        other = partner(me, step, wide)
        rows = pl.ds(pl.multiple_of(other * chunk, chunk), chunk)

        @pl.loop(0, 2 * KXM // COLS)
        def _(t):
            cols = pl.ds(pl.multiple_of(t * COLS, COLS), COLS)
            acc[:, cols] += jnp.dot(
                recv[other], tab[rows, cols], preferred_element_type=jnp.float32
            )

        return carry

    lax.fori_loop(1, wide, chunk_step, 0)

    norm_scale = 1.0 / math.sqrt(NXG)

    @pl.loop(0, KXM // 256)
    def _(t):
        cc = pl.ds(pl.multiple_of(t * 256, 256), 256)
        ss = pl.ds(pl.multiple_of(KXM + t * 256, 256), 256)
        kx = (
            lax.broadcasted_iota(jnp.int32, (1, 256), 1) + t * 256 - KXM // 2
        ).astype(jnp.float32) * spacing
        n = levels
        fx_real = (acc[0:n, cc] + acc[n:2 * n, ss]) * norm_scale
        fx_imag = (acc[n:2 * n, cc] - acc[0:n, ss]) * norm_scale
        fg_real = (acc[2 * n:3 * n, cc] + acc[3 * n:4 * n, ss]) * norm_scale
        fg_imag = (acc[3 * n:4 * n, cc] - acc[2 * n:3 * n, ss]) * norm_scale
        part[0, :, cc] = kx * fx_imag - fg_real
        part[1, :, cc] = -kx * fx_real - fg_imag

    def down_step(i, carry):
        value = (part[:, pl.ds(i, 1), :] + carry) * coef[pl.ds(i, 1), :][None]
        part[:, pl.ds(i, 1), :] = value
        return value

    zero_pair = jnp.zeros((2, 1, KXM), jnp.float32)
    lax.fori_loop(0, levels, down_step, zero_pair, unroll=4)

    def up_step(j, carry):
        i = levels - 1 - j
        value = part[:, pl.ds(i, 1), :] + coef[pl.ds(i, 1), :][None] * carry
        part[:, pl.ds(i, 1), :] = value
        return value

    lax.fori_loop(0, levels, up_step, zero_pair, unroll=4)

    ends[block, 0:2, :] = part[:, 0, :]
    ends[block, 2:4, :] = part[:, levels - 1, :]

    def end_copy(step, slot):
        return pltpu.make_async_remote_copy(
            src_ref=ends.at[slot],
            dst_ref=ends.at[slot],
            send_sem=end_send.at[step],
            recv_sem=end_recv.at[step],
            device_id={"lev": (block + step) % lev},
            device_id_type=MESH,
        )

    for step in range(1, lev):
        end_copy(step, block).start()
    for step in range(1, lev):
        end_copy(step, (block + lev - step) % lev).wait_recv()

    near, far = from_lo[0:1, :], from_lo[levels - 1:levels, :]
    value, ratio = ends[0, 2:4, :], near
    values, ratios, inverses = [value], [ratio], [None]
    for b in range(1, lev):
        inverse = 1.0 / (1.0 - near * ratio)
        lead = far * ratio * inverse
        first = ends[b, 0:2, :] + near * value
        value = ends[b, 2:4, :] + far * value + lead * first
        ratio = near + lead * far
        values.append(value)
        ratios.append(ratio)
        inverses.append(inverse)
    follow = jnp.zeros((2, KXM), jnp.float32)
    first_val[lev] = follow
    last_val[0] = follow
    for b in range(lev - 1, 0, -1):
        follow = inverses[b] * (ends[b, 0:2, :] + near * values[b - 1] + far * follow)
        first_val[b] = follow
        last_val[b] = values[b - 1] + ratios[b - 1] * follow
    below = last_val[block]
    above = first_val[block + 1]
    for c in range(2):
        out_ref[c] = part[c] + from_lo[...] * below[c:c + 1] + from_hi[...] * above[c:c + 1]

    to_prev.wait_send()
    to_next.wait_send()
    for step in range(1, wide):
        line_copy(step, 0).wait_send()
        line_copy(step, 1).wait_send()
    for step in range(1, lev):
        end_copy(step, block).wait_send()


def solution(mesh):
    wide, lev = mesh.shape["wide"], mesh.shape["lev"]
    tables = make_tables()

    def local(nonlinear):
        _, _, levels, rows_ky, chunk = nonlinear.shape
        rows = levels * rows_ky
        halo_rows = max(16, rows_ky)
        f32, bf16 = jnp.float32, jnp.bfloat16
        dma = pltpu.SemaphoreType.DMA
        pressure = pl.pallas_call(
            functools.partial(kernel, wide, lev, rows_ky, levels),
            out_shape=jax.ShapeDtypeStruct((2, levels, KXM), f32),
            in_specs=[
                pl.BlockSpec(memory_space=pltpu.VMEM),
                pl.BlockSpec(memory_space=pl.ANY),
            ],
            out_specs=pl.BlockSpec(memory_space=pltpu.VMEM),
            scratch_shapes=[
                pltpu.VMEM((NXG, 2 * KXM), bf16),
                pltpu.VMEM((wide, 4 * levels, chunk), bf16),
                pltpu.VMEM((wide, 4 * levels, chunk), bf16),
                pltpu.VMEM((2, halo_rows, chunk), bf16),
                pltpu.VMEM((2, halo_rows, chunk), bf16),
                pltpu.VMEM((2, rows + 2 * rows_ky, chunk), f32),
                pltpu.VMEM((4 * levels, 2 * KXM), f32),
                pltpu.VMEM((levels, KXM), f32),
                pltpu.VMEM((levels, KXM), f32),
                pltpu.VMEM((levels, KXM), f32),
                pltpu.VMEM((2, levels, KXM), f32),
                pltpu.VMEM((lev, 8, KXM), f32),
                pltpu.VMEM((lev + 1, 2, KXM), f32),
                pltpu.VMEM((lev + 1, 2, KXM), f32),
                dma((8,)),
                dma((2,)),
                dma((2,)),
                dma((2, wide)),
                dma((2, wide)),
                dma((lev,)),
                dma((lev,)),
            ],
            compiler_params=pltpu.CompilerParams(
                collective_id=0, has_side_effects=True, vmem_limit_bytes=56 * 2**20
            ),
            cost_estimate=pl.CostEstimate(
                flops=2 * 4 * levels * NXG * 2 * KXM,
                bytes_accessed=NXG * 2 * KXM * 2 + 4 * rows * chunk * 2,
                transcendentals=0,
            ),
        )(nonlinear.reshape(3, 2, rows, chunk), jnp.asarray(tables))
        return pressure.reshape(2, levels, 1, KXM)

    placed = (P(None, None, "lev", None, "wide"),)
    return jax.shard_map(
        local, mesh=mesh, in_specs=placed, out_specs=P(None, "lev", "wide", None), check_vma=False
    )
```

time: 549 us -> 71.8 us (0.13); the launches traced: 542 us -> 71.6 us
  matrix products: 198 us -> 0 us
  other arithmetic: 164 us -> 0 us
  waiting for transfers between devices: 70.6 us -> 0 us
  Pallas kernels: 0 us -> 68.8 us
  local copies, waits for them, and re-layouts: 66.6 us -> 2.82 us
  blocking collectives: 23.9 us -> 0 us
  starting transfers between devices: 15.5 us -> 0 us
    dot_general x2 -> x0, matrix products: 198 us -> none  [the longest x1 105 us: spectral_source(): jnp.dot(flat_rows, sine, preferred_element_type=jnp.float32)]
    dynamic_update_slice x201 -> x0, other arithmetic: 154 us -> none  [the longest x189 153 us: tridiag_sweep(): _, (inverses, reduced) = lax.scan(tridiag_forward_step, initial, source)]
    all_to_all x1 -> x0, waiting for transfers between devices: 70.6 us -> none  [local(): lax.all_to_all(nonlinear, 'wide', split_axis=3, concat_axis=4, tiled=True)]
    pallas_call x0 -> x1, Pallas kernels: none -> 68.8 us  [local(): pl.pallas_call(functools.partial(kernel, wide, lev, rows_ky, levels), out...]
    dynamic_slice x68 -> x0, local copies, waits for them, and re-layouts: 45.2 us -> none  [the longest x63 45.1 us: tridiag_sweep(): lax.scan(tridiag_backward_step, jnp.zeros_like(source[0]), (inverses, red...]
    all_gather x4 -> x0, blocking collectives: 23.9 us -> none  [the longest x1 8.25 us: local(): lax.all_gather(lower_coef[None], 'lev', axis=0, tiled=True)]
    ppermute x5 -> x0, starting transfers between devices: 8.2 us -> none  [the longest x3 3.88 us: from_behind(): return lax.ppermute(block, axis, route)]
    all_to_all x1 -> x0, starting transfers between devices: 7.28 us -> none  [local(): lax.all_to_all(nonlinear, 'wide', split_axis=3, concat_axis=4, tiled=True)]
  transfers between devices with their start and end apart: 6 -> 0, of which waited for: 1 -> 0; matrix products, arithmetic and copies ran while one was open for 2% -> 0% of each run, Pallas kernels for 0% -> 0%
where the time goes in v1:
time: 71.8 us; the launch traced here: 71.6 us
  Pallas kernels  68.8 us (96%)
  local copies, waits for them, and re-layouts  2.82 us (4%)
    pallas_call x1, Pallas kernels, local(): pl.pallas_call(functools.partial(kernel, wide, lev, rows_ky, levels), out...  68.8 us
    reshape x1, local copies, waits for them, and re-layouts, local(): return pressure.reshape(2, levels, 1, KXM)  2.82 us

profile of v1, /device:TPU:0, one launch (start us, length us, event | category | flops | bytes accessed | tf_op | source)
XLA Modules:
  0.0 71.6 jit_solution(10958100980209676375)
XLA Ops:
  0.0 68.8 %shard_map.28 = f32[2,64,1536]{2,1,0:T(8,128)} custom-call(bf16[3,2,512,512]{3,2,1,0:T(8,128)(2,1)} %bitcast.2, bf16[4096,3072]{1,0:T(8,128)(2,1)} %constant.2.clone.tab_ref), custom_call_target="tpu_custom_call" | custom-call | flops 6442450944 | bytes 27262976 | tf_op jit(solution)/shard_map/pallas_call | solution.py:316
  68.8 2.8 %copy.3 = f32[2,64,1,1536]{3,2,1,0:T(1,128)} copy(f32[2,64,1,1536]{3,1,0,2:T(8,128)} %bitcast.3) | data formatting | bytes 1572864 | tf_op jit(solution)/shard_map/reshape | solution.py:356

commit v2 on v1

--- a/solution.py
+++ b/solution.py
@@ -67,6 +67,48 @@
         pl.semaphore_signal(
             barrier, inc=1, device_id={"lev": (block + step) % lev}, device_id_type=MESH
         )
+    out_row = lax.broadcasted_iota(jnp.int32, (group_rows, group_rows), 0)
+    in_row = lax.broadcasted_iota(jnp.int32, (group_rows, group_rows), 1)
+    wanted = (out_row % group_levels) * rows_ky + out_row // group_levels
+    shuffle = jnp.where(in_row == wanted, 1.0, 0.0).astype(jnp.bfloat16)
+
+    def place(values, first):
+        moved = jnp.dot(shuffle, values, preferred_element_type=jnp.float32).astype(jnp.bfloat16)
+        for ky in range(rows_ky):
+            send[ky, first:first + group_levels, :] = moved[
+                ky * group_levels:(ky + 1) * group_levels
+            ]
+
+    def line_copy(step, which):
+        other = partner(me, step, wide)
+        rows = pl.ds(which * half, half)
+        return pltpu.make_async_remote_copy(
+            src_ref=send.at[other, rows],
+            dst_ref=recv.at[me, rows],
+            send_sem=send_sem.at[which, step],
+            recv_sem=recv_sem.at[which, step],
+            device_id={"wide": other},
+            device_id_type=MESH,
+        )
+
+    def line_arrival(step, which):
+        other = partner(me, step, wide)
+        rows = pl.ds(which * half, half)
+        return pltpu.make_async_remote_copy(
+            src_ref=send.at[other, rows],
+            dst_ref=recv.at[other, rows],
+            send_sem=send_sem.at[which, step],
+            recv_sem=recv_sem.at[which, step],
+            device_id={"wide": other},
+            device_id_type=MESH,
+        )
+
+    for c in range(2):
+        for g in range(groups):
+            place(
+                x_ref[0, c, g * group_rows:(g + 1) * group_rows, :],
+                c * levels + g * group_levels,
+            )
     pl.semaphore_wait(barrier, wide + lev - 2)
 
     to_prev = pltpu.make_async_remote_copy(
@@ -88,49 +130,9 @@
     to_prev.start()
     to_next.start()
 
-    out_row = lax.broadcasted_iota(jnp.int32, (group_rows, group_rows), 0)
-    in_row = lax.broadcasted_iota(jnp.int32, (group_rows, group_rows), 1)
-    wanted = (out_row % group_levels) * rows_ky + out_row // group_levels
-    shuffle = jnp.where(in_row == wanted, 1.0, 0.0).astype(jnp.bfloat16)
-
-    def place(values, first):
-        moved = jnp.dot(shuffle, values, preferred_element_type=jnp.float32).astype(jnp.bfloat16)
-        for ky in range(rows_ky):
-            send[ky, first:first + group_levels, :] = moved[
-                ky * group_levels:(ky + 1) * group_levels
-            ]
-
-    def line_copy(step, which):
-        other = partner(me, step, wide)
-        rows = pl.ds(which * half, half)
-        return pltpu.make_async_remote_copy(
-            src_ref=send.at[other, rows],
-            dst_ref=recv.at[me, rows],
-            send_sem=send_sem.at[which, step],
-            recv_sem=recv_sem.at[which, step],
-            device_id={"wide": other},
-            device_id_type=MESH,
-        )
-
-    def line_arrival(step, which):
-        other = partner(me, step, wide)
-        rows = pl.ds(which * half, half)
-        return pltpu.make_async_remote_copy(
-            src_ref=send.at[other, rows],
-            dst_ref=recv.at[other, rows],
-            send_sem=send_sem.at[which, step],
-            recv_sem=recv_sem.at[which, step],
-            device_id={"wide": other},
-            device_id_type=MESH,
-        )
-
-    for c in range(2):
-        for g in range(groups):
-            place(
-                x_ref[0, c, g * group_rows:(g + 1) * group_rows, :],
-                c * levels + g * group_levels,
-            )
-    for step in range(wide - 1, 0, -1):
+    far_steps = range(wide - 1, wide // 2 - 1, -1)
+    near_steps = range(wide // 2 - 1, 0, -1)
+    for step in far_steps:
         line_copy(step, 0).start()
 
     for i in range(tab_parts):
@@ -157,7 +159,10 @@
             slope = (upper - lower) * 0.5
             mixed = slope - turned if c == 0 else slope + turned
             place(mixed.astype(jnp.bfloat16), half + c * levels + g * group_levels)
-    for step in range(wide - 1, 0, -1):
+    for step in far_steps:
+        line_copy(step, 1).start()
+    for step in near_steps:
+        line_copy(step, 0).start()
         line_copy(step, 1).start()
 
     kx_scaled = (
@@ -217,43 +222,42 @@
 
         return carry
 
-    lax.fori_loop(1, wide, chunk_step, 0)
-
+    lax.fori_loop(1, wide - 1, chunk_step, 0)
+
+    line_arrival(wide - 1, 0).wait_recv()
+    line_arrival(wide - 1, 1).wait_recv()
+    last = partner(me, wide - 1, wide)
+    last_rows = pl.ds(pl.multiple_of(last * chunk, chunk), chunk)
     norm_scale = 1.0 / math.sqrt(NXG)
 
     @pl.loop(0, KXM // 256)
     def _(t):
         cc = pl.ds(pl.multiple_of(t * 256, 256), 256)
         ss = pl.ds(pl.multiple_of(KXM + t * 256, 256), 256)
+        lines = recv[last]
+        with_cos = acc[:, cc] + jnp.dot(
+            lines, tab[last_rows, cc], preferred_element_type=jnp.float32
+        )
+        with_sin = acc[:, ss] + jnp.dot(
+            lines, tab[last_rows, ss], preferred_element_type=jnp.float32
+        )
         kx = (
             lax.broadcasted_iota(jnp.int32, (1, 256), 1) + t * 256 - KXM // 2
         ).astype(jnp.float32) * spacing
         n = levels
-        fx_real = (acc[0:n, cc] + acc[n:2 * n, ss]) * norm_scale
-        fx_imag = (acc[n:2 * n, cc] - acc[0:n, ss]) * norm_scale
-        fg_real = (acc[2 * n:3 * n, cc] + acc[3 * n:4 * n, ss]) * norm_scale
-        fg_imag = (acc[3 * n:4 * n, cc] - acc[2 * n:3 * n, ss]) * norm_scale
-        part[0, :, cc] = kx * fx_imag - fg_real
-        part[1, :, cc] = -kx * fx_real - fg_imag
-
-    def down_step(i, carry):
-        value = (part[:, pl.ds(i, 1), :] + carry) * coef[pl.ds(i, 1), :][None]
-        part[:, pl.ds(i, 1), :] = value
-        return value
-
-    zero_pair = jnp.zeros((2, 1, KXM), jnp.float32)
-    lax.fori_loop(0, levels, down_step, zero_pair, unroll=4)
-
-    def up_step(j, carry):
-        i = levels - 1 - j
-        value = part[:, pl.ds(i, 1), :] + coef[pl.ds(i, 1), :][None] * carry
-        part[:, pl.ds(i, 1), :] = value
-        return value
-
-    lax.fori_loop(0, levels, up_step, zero_pair, unroll=4)
-
-    ends[block, 0:2, :] = part[:, 0, :]
-    ends[block, 2:4, :] = part[:, levels - 1, :]
+        fx_real = (with_cos[0:n] + with_sin[n:2 * n]) * norm_scale
+        fx_imag = (with_cos[n:2 * n] - with_sin[0:n]) * norm_scale
+        fg_real = (with_cos[2 * n:3 * n] + with_sin[3 * n:4 * n]) * norm_scale
+        fg_imag = (with_cos[3 * n:4 * n] - with_sin[2 * n:3 * n]) * norm_scale
+        source_real = kx * fx_imag - fg_real
+        source_imag = -kx * fx_real - fg_imag
+        part[0, :, cc] = source_real
+        part[1, :, cc] = source_imag
+        low, high = from_lo[:, cc], from_hi[:, cc]
+        ends[block, 0:1, cc] = jnp.sum(low * source_real, axis=0, keepdims=True)
+        ends[block, 1:2, cc] = jnp.sum(low * source_imag, axis=0, keepdims=True)
+        ends[block, 2:3, cc] = jnp.sum(high * source_real, axis=0, keepdims=True)
+        ends[block, 3:4, cc] = jnp.sum(high * source_imag, axis=0, keepdims=True)
 
     def end_copy(step, slot):
         return pltpu.make_async_remote_copy(
@@ -267,6 +271,23 @@
 
     for step in range(1, lev):
         end_copy(step, block).start()
+
+    def down_step(i, carry):
+        value = (part[:, pl.ds(i, 1), :] + carry) * coef[pl.ds(i, 1), :][None]
+        part[:, pl.ds(i, 1), :] = value
+        return value
+
+    zero_pair = jnp.zeros((2, 1, KXM), jnp.float32)
+    lax.fori_loop(0, levels, down_step, zero_pair, unroll=4)
+
+    def up_step(j, carry):
+        i = levels - 1 - j
+        value = part[:, pl.ds(i, 1), :] + coef[pl.ds(i, 1), :][None] * carry
+        part[:, pl.ds(i, 1), :] = value
+        return value
+
+    lax.fori_loop(0, levels, up_step, zero_pair, unroll=4)
+
     for step in range(1, lev):
         end_copy(step, (block + lev - step) % lev).wait_recv()
 
@@ -291,8 +312,16 @@
         last_val[b] = values[b - 1] + ratios[b - 1] * follow
     below = last_val[block]
     above = first_val[block + 1]
-    for c in range(2):
-        out_ref[c] = part[c] + from_lo[...] * below[c:c + 1] + from_hi[...] * above[c:c + 1]
+    tiles = KXM // 128
+    for c in range(2):
+        for j in range(tiles):
+            at = slice(j * 128, (j + 1) * 128)
+            solved = (
+                part[c, :, at]
+                + from_lo[:, at] * below[c:c + 1, at]
+                + from_hi[:, at] * above[c:c + 1, at]
+            )
+            out_ref[pl.ds(c * levels * tiles + j, levels, stride=tiles), :] = solved
 
     to_prev.wait_send()
     to_next.wait_send()
@@ -315,7 +344,7 @@
         dma = pltpu.SemaphoreType.DMA
         pressure = pl.pallas_call(
             functools.partial(kernel, wide, lev, rows_ky, levels),
-            out_shape=jax.ShapeDtypeStruct((2, levels, KXM), f32),
+            out_shape=jax.ShapeDtypeStruct((2 * levels * KXM // 128, 128), f32),
             in_specs=[
                 pl.BlockSpec(memory_space=pltpu.VMEM),
                 pl.BlockSpec(memory_space=pl.ANY),

time: 71.8 us -> 69.5 us (0.968)
  Pallas kernels: 68.8 us -> 67.2 us
  local copies, waits for them, and re-layouts: 2.82 us -> 2.09 us
    reshape x1 -> x0, local copies, waits for them, and re-layouts: 2.82 us -> none  [local(): return pressure.reshape(2, levels, 1, KXM)]
    unnamed x0 -> x1, local copies, waits for them, and re-layouts: none -> 2.09 us
    pallas_call x1, Pallas kernels: 68.8 us -> 67.2 us  [local(): pl.pallas_call(functools.partial(kernel, wide, lev, rows_ky, levels), out...]
where the time goes in v2:
time: 69.5 us; the launch traced here: 69.3 us
  Pallas kernels  67.2 us (97%)
  local copies, waits for them, and re-layouts  2.09 us (3%)
    pallas_call x1, Pallas kernels, local(): pl.pallas_call(functools.partial(kernel, wide, lev, rows_ky, levels), out...  67.2 us
    unnamed x1, local copies, waits for them, and re-layouts  2.09 us

profile of v2, /device:TPU:0, one launch (start us, length us, event | category | flops | bytes accessed | tf_op | source)
XLA Modules:
  0.0 69.3 jit_solution(1747696864808498969)
XLA Ops:
  0.0 67.2 %shard_map.28 = f32[1536,128]{1,0:T(8,128)} custom-call(bf16[3,2,512,512]{3,2,1,0:T(8,128)(2,1)} %bitcast.2, bf16[4096,3072]{1,0:T(8,128)(2,1)} %constant.2.clone.tab_ref), custom_call_target="tpu_custom_call" | custom-call | flops 6442450944 | bytes 27262976 | tf_op jit(solution)/shard_map/pallas_call | solution.py:345
  67.2 2.1 %copy.5 = f32[2,64,1,1536]{3,2,1,0:T(1,128)} copy(f32[2,64,1,1536]{3,2,1,0:T(1,128)} %bitcast.3) | data formatting | bytes 1572864

commit v3 on v2

--- a/solution.py
+++ b/solution.py
@@ -37,7 +37,7 @@
 def kernel(
     wide, lev, rows_ky, levels,
     x_ref, tab_ref, out_ref,
-    tab, send, recv, halo_lo, halo_hi, zpad, acc, coef, from_lo, from_hi, part,
+    tab, send, recv, halo_lo, halo_hi, zpad, acc, coef, from_lo, from_hi, part, dense,
     ends, last_val, first_val,
     tab_sem, halo_send, halo_recv, send_sem, recv_sem, end_send, end_recv,
 ):
@@ -130,9 +130,12 @@
     to_prev.start()
     to_next.start()
 
-    far_steps = range(wide - 1, wide // 2 - 1, -1)
+    quarter = wide // 4
+    same = (me // (2 * quarter) + me // quarter + 1) % 2
+    end_steps = [2 * quarter + same * quarter + i for i in range(quarter)]
+    mid_steps = [2 * quarter + (1 - same) * quarter + i for i in range(quarter)]
     near_steps = range(wide // 2 - 1, 0, -1)
-    for step in far_steps:
+    for step in end_steps:
         line_copy(step, 0).start()
 
     for i in range(tab_parts):
@@ -159,11 +162,12 @@
             slope = (upper - lower) * 0.5
             mixed = slope - turned if c == 0 else slope + turned
             place(mixed.astype(jnp.bfloat16), half + c * levels + g * group_levels)
-    for step in far_steps:
+    for step in end_steps:
         line_copy(step, 1).start()
-    for step in near_steps:
-        line_copy(step, 0).start()
-        line_copy(step, 1).start()
+    for steps in (mid_steps, near_steps):
+        for step in steps:
+            line_copy(step, 0).start()
+            line_copy(step, 1).start()
 
     kx_scaled = (
         lax.broadcasted_iota(jnp.int32, (1, KXM), 1) - KXM // 2
@@ -194,6 +198,13 @@
         return low, high
 
     lax.fori_loop(0, levels, unit_step, (zeros, ones))
+
+    tiles = KXM // 128
+    deep = 2 * tiles
+    for j in range(tiles):
+        column = coef[:, j * 128:(j + 1) * 128]
+        for c in range(2):
+            dense[pl.ds(c * tiles + j, levels, stride=deep), :] = column
 
     for i in range(tab_parts):
         tab_copy(i).wait()
@@ -251,8 +262,10 @@
         fg_imag = (with_cos[3 * n:4 * n] - with_sin[2 * n:3 * n]) * norm_scale
         source_real = kx * fx_imag - fg_real
         source_imag = -kx * fx_real - fg_imag
-        part[0, :, cc] = source_real
-        part[1, :, cc] = source_imag
+        for j in range(2):
+            at = slice(j * 128, (j + 1) * 128)
+            part[pl.ds(2 * t + j, n, stride=deep), :] = source_real[:, at]
+            part[pl.ds(tiles + 2 * t + j, n, stride=deep), :] = source_imag[:, at]
         low, high = from_lo[:, cc], from_hi[:, cc]
         ends[block, 0:1, cc] = jnp.sum(low * source_real, axis=0, keepdims=True)
         ends[block, 1:2, cc] = jnp.sum(low * source_imag, axis=0, keepdims=True)
@@ -273,20 +286,21 @@
         end_copy(step, block).start()
 
     def down_step(i, carry):
-        value = (part[:, pl.ds(i, 1), :] + carry) * coef[pl.ds(i, 1), :][None]
-        part[:, pl.ds(i, 1), :] = value
+        rows = pl.ds(pl.multiple_of(i * deep, 8), deep)
+        value = (part[rows, :] + carry) * dense[rows, :]
+        part[rows, :] = value
         return value
 
-    zero_pair = jnp.zeros((2, 1, KXM), jnp.float32)
-    lax.fori_loop(0, levels, down_step, zero_pair, unroll=4)
+    zero_level = jnp.zeros((deep, 128), jnp.float32)
+    lax.fori_loop(0, levels, down_step, zero_level, unroll=8)
 
     def up_step(j, carry):
-        i = levels - 1 - j
-        value = part[:, pl.ds(i, 1), :] + coef[pl.ds(i, 1), :][None] * carry
-        part[:, pl.ds(i, 1), :] = value
+        rows = pl.ds(pl.multiple_of((levels - 1 - j) * deep, 8), deep)
+        value = part[rows, :] + dense[rows, :] * carry
+        part[rows, :] = value
         return value
 
-    lax.fori_loop(0, levels, up_step, zero_pair, unroll=4)
+    lax.fori_loop(0, levels, up_step, zero_level, unroll=8)
 
     for step in range(1, lev):
         end_copy(step, (block + lev - step) % lev).wait_recv()
@@ -312,12 +326,11 @@
         last_val[b] = values[b - 1] + ratios[b - 1] * follow
     below = last_val[block]
     above = first_val[block + 1]
-    tiles = KXM // 128
     for c in range(2):
         for j in range(tiles):
             at = slice(j * 128, (j + 1) * 128)
             solved = (
-                part[c, :, at]
+                part[pl.ds(c * tiles + j, levels, stride=deep), :]
                 + from_lo[:, at] * below[c:c + 1, at]
                 + from_hi[:, at] * above[c:c + 1, at]
             )
@@ -361,7 +374,8 @@
                 pltpu.VMEM((levels, KXM), f32),
                 pltpu.VMEM((levels, KXM), f32),
                 pltpu.VMEM((levels, KXM), f32),
-                pltpu.VMEM((2, levels, KXM), f32),
+                pltpu.VMEM((2 * levels * KXM // 128, 128), f32),
+                pltpu.VMEM((2 * levels * KXM // 128, 128), f32),
                 pltpu.VMEM((lev, 8, KXM), f32),
                 pltpu.VMEM((lev + 1, 2, KXM), f32),
                 pltpu.VMEM((lev + 1, 2, KXM), f32),

time: 69.5 us -> 61.9 us (0.89)
  the two profiles are of different devices: /device:TPU:0 before, /device:TPU:13 now
where the time goes in v3:
time: 61.9 us; the launch traced here: 61.7 us
  Pallas kernels  59.6 us (96%)
  local copies, waits for them, and re-layouts  2.09 us (3%)
    pallas_call x1, Pallas kernels, local(): pl.pallas_call(functools.partial(kernel, wide, lev, rows_ky, levels), out...  59.6 us
    unnamed x1, local copies, waits for them, and re-layouts  2.09 us

profile of v3, /device:TPU:13, one launch (start us, length us, event | category | flops | bytes accessed | tf_op | source)
XLA Modules:
  0.0 61.7 jit_solution(14251017218275914496)
XLA Ops:
  0.0 59.6 %shard_map.28 = f32[1536,128]{1,0:T(8,128)} custom-call(bf16[3,2,512,512]{3,2,1,0:T(8,128)(2,1)} %bitcast.2, bf16[4096,3072]{1,0:T(8,128)(2,1)} %constant.2.clone.tab_ref), custom_call_target="tpu_custom_call" | custom-call | flops 6442450944 | bytes 27262976 | tf_op jit(solution)/shard_map/pallas_call | solution.py:358
  59.6 2.1 %copy.5 = f32[2,64,1,1536]{3,2,1,0:T(1,128)} copy(f32[2,64,1,1536]{3,2,1,0:T(1,128)} %bitcast.3) | data formatting | bytes 1572864

commit v4 on v3

--- a/solution.py
+++ b/solution.py
@@ -134,7 +134,11 @@
     same = (me // (2 * quarter) + me // quarter + 1) % 2
     end_steps = [2 * quarter + same * quarter + i for i in range(quarter)]
     mid_steps = [2 * quarter + (1 - same) * quarter + i for i in range(quarter)]
-    near_steps = range(wide // 2 - 1, 0, -1)
+    later_steps = []
+    for i in range(wide // 2 - 1):
+        later_steps.append(i + 1)
+        if i < quarter:
+            later_steps.append(mid_steps[i])
     for step in end_steps:
         line_copy(step, 0).start()
 
@@ -164,10 +168,9 @@
             place(mixed.astype(jnp.bfloat16), half + c * levels + g * group_levels)
     for step in end_steps:
         line_copy(step, 1).start()
-    for steps in (mid_steps, near_steps):
-        for step in steps:
-            line_copy(step, 0).start()
-            line_copy(step, 1).start()
+    for step in later_steps:
+        line_copy(step, 0).start()
+        line_copy(step, 1).start()
 
     kx_scaled = (
         lax.broadcasted_iota(jnp.int32, (1, KXM), 1) - KXM // 2
@@ -218,7 +221,11 @@
             send[me], tab[pl.ds(own_at, chunk), cols], preferred_element_type=jnp.float32
         )
 
-    def chunk_step(step, carry):
+    def nth_step(n):
+        return (n - 1 + same * (wide // 2 - 1)) % (wide - 1) + 1
+
+    def chunk_step(n, carry):
+        step = nth_step(n)
         line_arrival(step, 0).wait_recv()
         line_arrival(step, 1).wait_recv()
         other = partner(me, step, wide)
@@ -235,9 +242,10 @@
 
     lax.fori_loop(1, wide - 1, chunk_step, 0)
 
-    line_arrival(wide - 1, 0).wait_recv()
-    line_arrival(wide - 1, 1).wait_recv()
-    last = partner(me, wide - 1, wide)
+    last_step = nth_step(wide - 1)
+    line_arrival(last_step, 0).wait_recv()
+    line_arrival(last_step, 1).wait_recv()
+    last = partner(me, last_step, wide)
     last_rows = pl.ds(pl.multiple_of(last * chunk, chunk), chunk)
     norm_scale = 1.0 / math.sqrt(NXG)
 

time: 61.9 us -> 62.3 us (level)
  the two profiles are of different devices: /device:TPU:13 before, /device:TPU:0 now
where the time goes in v4:
time: 62.3 us; the launch traced here: 62.1 us
  Pallas kernels  60 us (96%)
  local copies, waits for them, and re-layouts  2.09 us (3%)
    pallas_call x1, Pallas kernels, local(): pl.pallas_call(functools.partial(kernel, wide, lev, rows_ky, levels), out...  60 us
    unnamed x1, local copies, waits for them, and re-layouts  2.09 us

profile of v4, /device:TPU:0, one launch (start us, length us, event | category | flops | bytes accessed | tf_op | source)
XLA Modules:
  0.0 62.1 jit_solution(14198328977874419887)
XLA Ops:
  0.0 60.0 %shard_map.28 = f32[1536,128]{1,0:T(8,128)} custom-call(bf16[3,2,512,512]{3,2,1,0:T(8,128)(2,1)} %bitcast.2, bf16[4096,3072]{1,0:T(8,128)(2,1)} %constant.2.clone.tab_ref), custom_call_target="tpu_custom_call" | custom-call | flops 6442450944 | bytes 27262976 | tf_op jit(solution)/shard_map/pallas_call | solution.py:366
  60.0 2.1 %copy.5 = f32[2,64,1,1536]{3,2,1,0:T(1,128)} copy(f32[2,64,1,1536]{3,2,1,0:T(1,128)} %bitcast.3) | data formatting | bytes 1572864

commit v5 on v3

--- a/solution.py
+++ b/solution.py
@@ -343,6 +343,10 @@
         line_copy(step, 1).wait_send()
     for step in range(1, lev):
         end_copy(step, block).wait_send()
+
+
+def hand_over(x_ref, out_ref):
+    out_ref[...] = x_ref[...]
 
 
 def solution(mesh):
@@ -396,6 +400,9 @@
                 transcendentals=0,
             ),
         )(nonlinear.reshape(3, 2, rows, chunk), jnp.asarray(tables))
+        pressure = pl.pallas_call(
+            hand_over, out_shape=jax.ShapeDtypeStruct(pressure.shape, f32)
+        )(pressure)
         return pressure.reshape(2, levels, 1, KXM)
 
     placed = (P(None, None, "lev", None, "wide"),)

time: 61.9 us -> 61.9 us (level)
  Pallas kernels: 59.6 us -> 61.7 us
  local copies, waits for them, and re-layouts: 2.09 us -> 0 us
    unnamed x1 -> x0, local copies, waits for them, and re-layouts: 2.09 us -> none
    pallas_call x0 -> x1, Pallas kernels: none -> 2.06 us  [local(): pl.pallas_call(hand_over, out_shape=jax.ShapeDtypeStruct(pressure.shape,...]
where the time goes in v5:
time: 61.9 us; the launch traced here: 61.7 us
  Pallas kernels  61.7 us (100%)
    pallas_call x1, Pallas kernels, local(): pl.pallas_call(functools.partial(kernel, wide, lev, rows_ky, levels), out...  59.6 us
    pallas_call x1, Pallas kernels, local(): pl.pallas_call(hand_over, out_shape=jax.ShapeDtypeStruct(pressure.shape,...  2.06 us

profile of v5, /device:TPU:13, one launch (start us, length us, event | category | flops | bytes accessed | tf_op | source)
XLA Modules:
  0.0 61.7 jit_solution(12730390730778042648)
XLA Ops:
  0.0 59.6 %shard_map.28.x_ref = f32[1536,128]{1,0:T(8,128)} custom-call(bf16[3,2,512,512]{3,2,1,0:T(8,128)(2,1)} %bitcast.2, bf16[4096,3072]{1,0:T(8,128)(2,1)} %constant.2.clone.tab_ref), custom_call_target="tpu_custom_call" | custom-call | flops 6442450944 | bytes 27262976 | tf_op jit(solution)/shard_map/pallas_call | solution.py:362
  59.6 2.1 %shard_map.29 = f32[1536,128]{1,0:T(8,128)} custom-call(f32[1536,128]{1,0:T(8,128)} %shard_map.28.x_ref), custom_call_target="tpu_custom_call" | custom-call | tf_op jit(solution)/shard_map/pallas_call | solution.py:403
